TPU v7x, 32 devices: a whole 2x2x4 slice. The times are simulated.
32 devices in a mesh: dp: 16 (over z, y, x), tensor: 2 (over core).
Axes of the slice: x: 2, y: 2, z: 4, core: 2. Of those that a mesh axis runs over, the one named last changes fastest.
Arguments:
- tokens: float32 [16384, 768], P(('dp', 'tensor')), may hold values from -6 to 6
- offsets: int32 [16, 16], P('dp'), may hold values from 0 to 1024, as said below
- w_qkv: bfloat16 [768, 3, 768], P('dp', None, 'tensor'), may hold values from -0.21875 to 0.21875
- w_attn_out: bfloat16 [768, 768], P('tensor', 'dp'), may hold values from -1.75 to 1.75
- w_in: bfloat16 [768, 2, 1152], P('dp', None, 'tensor'), may hold values from -0.21875 to 0.21875
- w_mlp_out: bfloat16 [1152, 768], P('tensor', 'dp'), may hold values from -0.1875 to 0.1875
- gain_attn: bfloat16 [768], P('dp'), may hold values from 0.099609375 to 1.8984375
- gain_mlp: bfloat16 [768], P('dp'), may hold values from 0.099609375 to 1.8984375
- cotangent: float32 [16384, 768], P(('dp', 'tensor')), may hold values from -6 to 6
Outputs:
- outputs: float32 [16384, 768], P(('dp', 'tensor'))
- grad_tokens: float32 [16384, 768], P(('dp', 'tensor'))
- grad_w_qkv: float32 [768, 3, 768], P('dp', None, 'tensor')
- grad_w_attn_out: float32 [768, 768], P('tensor', 'dp')
- grad_w_in: float32 [768, 2, 1152], P('dp', None, 'tensor')
- grad_w_mlp_out: float32 [1152, 768], P('tensor', 'dp')
- grad_gain_attn: float32 [768], P('dp')
- grad_gain_mlp: float32 [768], P('dp')
Inputs may be any that keep to these rules, and one draw needn't show every extreme that they name: `offsets`: each row holds the first tokens of 16 sequences of one group of 1024 tokens, rising from 0 and never falling (equal entries are empty sequences); a sequence ends where the next begins, the last at 1024. No sequence has more than 512 tokens; in every row one has exactly 512 and holds the group's tokens 512 - 1 and 512.
All inputs are finite; a program needn't handle non-finite values.
Results may differ from a plain program's by a relative error of at most 0.018.
Values may be sent and summed in bfloat16 or wider, within the bound.
A program may use at most 128 MiB of HBM per device.

v0:
```python
import math
import jax
import jax.numpy as jnp
from jax import lax
from jax.sharding import PartitionSpec as P

HEAD_DIM = 64
EPSILON = 1e-05
ROPE_BASE = 160000.0
NEGATIVE = -1e30


def seq_starts(offset_row, count_rows):
    position = jnp.arange(count_rows, dtype=jnp.int32)
    before = offset_row[None, :] <= position[:, None]
    return jnp.max(jnp.where(before, offset_row[None, :], 0), axis=1)


def rope_tables(starts):
    count_rows = starts.shape[0]
    position = jnp.arange(count_rows, dtype=jnp.int32) - starts
    half_dim = HEAD_DIM // 2
    inverse = jnp.power(
        jnp.float32(ROPE_BASE), -2.0 * jnp.arange(half_dim, dtype=jnp.float32) / HEAD_DIM
    )
    angles = position.astype(jnp.float32)[:, None] * inverse[None, :]
    return (jnp.cos(angles), jnp.sin(angles))


def rotate(head_rows, cosine_tab, sine_tab):
    half_dim = HEAD_DIM // 2
    first_half = head_rows[..., :half_dim]
    second = head_rows[..., half_dim:]
    cosine_b = cosine_tab[:, None, :]
    sine_b = sine_tab[:, None, :]
    return jnp.concatenate(
        [first_half * cosine_b - second * sine_b, second * cosine_b + first_half * sine_b], axis=-1
    )


def rotate_back(head_grads, cosine_tab, sine_tab):
    half_dim = HEAD_DIM // 2
    first_half = head_grads[..., :half_dim]
    second = head_grads[..., half_dim:]
    cosine_b = cosine_tab[:, None, :]
    sine_b = sine_tab[:, None, :]
    return jnp.concatenate(
        [first_half * cosine_b + second * sine_b, second * cosine_b - first_half * sine_b], axis=-1
    )


def layer_norm(inputs_v, gain_v):
    centre = inputs_v - jnp.mean(inputs_v, axis=-1, keepdims=True)
    spread = jnp.mean(centre * centre, axis=-1, keepdims=True)
    return centre * lax.rsqrt(spread + EPSILON) * gain_v


def exact_gelu(gate_in):
    return jax.nn.gelu(gate_in, approximate=False)


def fetch_attention(w_qkv, w_attn_out, gain_attn):
    return (
        lax.all_gather(w_qkv, "dp", axis=0, tiled=True),
        lax.all_gather(w_attn_out, "dp", axis=1, tiled=True),
        lax.all_gather(gain_attn, "dp", axis=0, tiled=True),
    )


def fetch_attention_again(w_qkv, w_attn_out, gain_attn):
    return (
        lax.all_gather(w_qkv, "dp", axis=0, tiled=True),
        lax.all_gather(w_attn_out, "dp", axis=1, tiled=True),
        lax.all_gather(gain_attn, "dp", axis=0, tiled=True),
    )


def fetch_mlp(w_in, w_mlp_out, gain_mlp):
    return (
        lax.all_gather(w_in, "dp", axis=0, tiled=True),
        lax.all_gather(w_mlp_out, "dp", axis=1, tiled=True),
        lax.all_gather(gain_mlp, "dp", axis=0, tiled=True),
    )


def fetch_mlp_again(w_in, w_mlp_out, gain_mlp):
    return (
        lax.all_gather(w_in, "dp", axis=0, tiled=True),
        lax.all_gather(w_mlp_out, "dp", axis=1, tiled=True),
        lax.all_gather(gain_mlp, "dp", axis=0, tiled=True),
    )


def spread_rows(local_rows):
    return lax.all_gather(local_rows, "tensor", axis=0, tiled=True)


def spread_grads(local_rows):
    return lax.all_gather(local_rows, "tensor", axis=0, tiled=True)


def collect_rows(inputs_all, weight_full, rows_here):

    def term_of(row_start, row_count):
        return jnp.dot(inputs_all, weight_full, preferred_element_type=jnp.float32)

    return lax.psum_scatter(
        term_of(jnp.int32(0), rows_here * lax.axis_size("tensor")).astype(jnp.bfloat16),
        "tensor",
        scatter_dimension=0,
        tiled=True,
    ).astype(jnp.float32)


def collect_grads(grads_all, weight_full, rows_here):

    def term_of(row_start, row_count):
        return jnp.einsum("tsk,dsk->td", grads_all, weight_full, preferred_element_type=jnp.float32)

    return lax.psum_scatter(
        term_of(jnp.int32(0), rows_here * lax.axis_size("tensor")).astype(jnp.bfloat16),
        "tensor",
        scatter_dimension=0,
        tiled=True,
    ).astype(jnp.float32)


def block_scores(query_block, start_block, key_rows, starts, scale_factor):
    raw_scores = (
        jnp.einsum("qhe,khe->hqk", query_block, key_rows, preferred_element_type=jnp.float32)
        * scale_factor
    )
    same_seq = start_block[:, None] == starts[None, :]
    return jnp.where(same_seq[None], raw_scores, NEGATIVE)


def attention_forward(queries, key_rows, values, starts, scale_factor):
    group_rows, heads_here, head_dim = queries.shape
    block_rows = min(512, group_rows)
    block_count = group_rows // block_rows

    def one_block(block_in):
        query_block, start_block = block_in
        masked = block_scores(query_block, start_block, key_rows, starts, scale_factor)
        row_max = jnp.max(masked, axis=-1, keepdims=True)
        exp_terms = jnp.exp(masked - row_max)
        row_total = jnp.sum(exp_terms, axis=-1, keepdims=True)
        softmax_w = exp_terms / row_total
        mixed_out = jnp.einsum(
            "hqk,khe->qhe",
            softmax_w.astype(jnp.bfloat16),
            values,
            preferred_element_type=jnp.float32,
        )
        return (mixed_out, (row_max + jnp.log(row_total))[..., 0])

    mixed_all, lse_stack = lax.map(
        one_block,
        (
            queries.reshape(block_count, block_rows, heads_here, head_dim),
            starts.reshape(block_count, block_rows),
        ),
    )
    return (mixed_all.reshape(group_rows, heads_here, head_dim), lse_stack)


def attention_backward(queries, key_rows, values, starts, lse_stack, grad_out, scale_factor):
    group_rows, heads_here, head_dim = queries.shape
    block_rows = min(512, group_rows)
    block_count = group_rows // block_rows

    def one_block(carry_in, block_in):
        grad_keys, grad_values = carry_in
        query_block, start_block, lse_block, grad_block = block_in
        masked = block_scores(query_block, start_block, key_rows, starts, scale_factor)
        softmax_w = jnp.exp(masked - lse_block[..., None])
        grad_values = grad_values + jnp.einsum(
            "hqk,qhe->khe",
            softmax_w.astype(jnp.bfloat16),
            grad_block,
            preferred_element_type=jnp.float32,
        )
        grad_probs = jnp.einsum(
            "qhe,khe->hqk", grad_block, values, preferred_element_type=jnp.float32
        )
        grad_scores = softmax_w * (
            grad_probs - jnp.sum(softmax_w * grad_probs, axis=-1, keepdims=True)
        )
        rounded = grad_scores.astype(jnp.bfloat16)
        grad_query = (
            jnp.einsum("hqk,khe->qhe", rounded, key_rows, preferred_element_type=jnp.float32)
            * scale_factor
        )
        grad_keys = (
            grad_keys
            + jnp.einsum("hqk,qhe->khe", rounded, query_block, preferred_element_type=jnp.float32)
            * scale_factor
        )
        return ((grad_keys, grad_values), grad_query)

    zero_grads = jnp.zeros((group_rows, heads_here, head_dim), jnp.float32)
    block_inputs = (
        queries.reshape(block_count, block_rows, heads_here, head_dim),
        starts.reshape(block_count, block_rows),
        lse_stack,
        grad_out.reshape(block_count, block_rows, heads_here, head_dim),
    )
    (grad_keys, grad_values), grad_queries = lax.scan(
        one_block, (zero_grads, zero_grads), block_inputs
    )
    return (grad_queries.reshape(group_rows, heads_here, head_dim), grad_keys, grad_values)


def shards(tokens, offsets, w_qkv, w_attn_out, w_in, w_mlp_out, gain_attn, gain_mlp, cotangent):
    rows_here = tokens.shape[0]
    group_rows = rows_here * lax.axis_size("tensor")
    scale_factor = 1.0 / math.sqrt(HEAD_DIM)
    starts = seq_starts(offsets[0], group_rows)
    cosine_tab, sine_tab = rope_tables(starts)
    qkv_full, attn_out_full, gain_one_low = fetch_attention(w_qkv, w_attn_out, gain_attn)
    gain_one = gain_one_low.astype(jnp.float32)
    normed_all = spread_rows(layer_norm(tokens, gain_one).astype(jnp.bfloat16))
    projected = jnp.einsum("td,dsk->tsk", normed_all, qkv_full, preferred_element_type=jnp.float32)
    width_here = projected.shape[2]
    heads_here = width_here // HEAD_DIM
    split_heads = projected.reshape(group_rows, 3, heads_here, HEAD_DIM)
    queries = rotate(split_heads[:, 0], cosine_tab, sine_tab).astype(jnp.bfloat16)
    key_rows = rotate(split_heads[:, 1], cosine_tab, sine_tab).astype(jnp.bfloat16)
    values = split_heads[:, 2].astype(jnp.bfloat16)
    mixed_all, lse_stack = attention_forward(queries, key_rows, values, starts, scale_factor)
    context = mixed_all.reshape(group_rows, width_here).astype(jnp.bfloat16)
    attended = collect_rows(context, attn_out_full, rows_here)
    hidden = tokens + attended
    mlp_in_full, mlp_out_full, gain_two_low = fetch_mlp(w_in, w_mlp_out, gain_mlp)
    gain_two = gain_two_low.astype(jnp.float32)
    mlp_normed = layer_norm(hidden, gain_two).astype(jnp.bfloat16)
    mlp_in_use, mlp_out_use = (mlp_in_full, mlp_out_full)
    mlp_rows = spread_rows(mlp_normed)
    gate_up = jnp.einsum("td,dsf->tsf", mlp_rows, mlp_in_use, preferred_element_type=jnp.float32)
    gate_part = gate_up[:, 0]
    up_part = gate_up[:, 1]
    activated = exact_gelu(gate_part)
    product_rows = (activated * up_part).astype(jnp.bfloat16)
    branch = collect_rows(product_rows, mlp_out_use, rows_here)
    outputs = hidden + branch
    mlp_in_back, mlp_out_back, gain_two_again = fetch_mlp_again(w_in, w_mlp_out, gain_mlp)
    gain_two_back = gain_two_again.astype(jnp.float32)
    grad_rows = spread_grads(cotangent.astype(jnp.bfloat16))
    grad_mlp_out = jnp.einsum(
        "tf,td->fd", product_rows, grad_rows, preferred_element_type=jnp.float32
    )
    grad_product = jnp.einsum(
        "td,fd->tf", grad_rows, mlp_out_back, preferred_element_type=jnp.float32
    )
    unused_out, gelu_pull = jax.vjp(exact_gelu, gate_part)
    grad_gate = gelu_pull(grad_product * up_part)[0]
    grad_up = grad_product * activated
    grad_gate_up = jnp.stack([grad_gate, grad_up], axis=1).astype(jnp.bfloat16)
    grad_mlp_in = jnp.einsum(
        "td,tsf->dsf", mlp_rows, grad_gate_up, preferred_element_type=jnp.float32
    )
    grad_normed_two = collect_grads(grad_gate_up, mlp_in_back, rows_here)
    unused_two, norm_pull_two = jax.vjp(layer_norm, hidden, gain_two_back)
    grad_hidden_norm, grad_gain_two = norm_pull_two(grad_normed_two)
    grad_hidden = cotangent + grad_hidden_norm
    mlp_sums = (
        lax.psum_scatter(grad_mlp_in, "dp", scatter_dimension=0, tiled=True),
        lax.psum_scatter(grad_mlp_out, "dp", scatter_dimension=1, tiled=True),
        lax.psum_scatter(grad_gain_two, "dp", scatter_dimension=0, tiled=True),
    )
    qkv_back, attn_out_back, gain_one_again = fetch_attention_again(w_qkv, w_attn_out, gain_attn)
    gain_one_back = gain_one_again.astype(jnp.float32)
    grad_hidden_rows = spread_grads(grad_hidden.astype(jnp.bfloat16))
    grad_attn_out = jnp.einsum(
        "te,td->ed", context, grad_hidden_rows, preferred_element_type=jnp.float32
    )
    grad_context = jnp.einsum(
        "td,ed->te", grad_hidden_rows, attn_out_back, preferred_element_type=jnp.float32
    ).astype(jnp.bfloat16)
    grad_queries, grad_keys, grad_values = attention_backward(
        queries,
        key_rows,
        values,
        starts,
        lse_stack,
        grad_context.reshape(group_rows, heads_here, HEAD_DIM),
        scale_factor,
    )
    grad_projected = jnp.stack(
        [
            rotate_back(grad_queries, cosine_tab, sine_tab),
            rotate_back(grad_keys, cosine_tab, sine_tab),
            grad_values,
        ],
        axis=1,
    )
    grad_projected = grad_projected.reshape(group_rows, 3, width_here).astype(jnp.bfloat16)
    grad_qkv = jnp.einsum(
        "td,tsk->dsk", normed_all, grad_projected, preferred_element_type=jnp.float32
    )
    grad_normed_one = collect_grads(grad_projected, qkv_back, rows_here)
    unused_one, norm_pull_one = jax.vjp(layer_norm, tokens, gain_one_back)
    grad_tokens_norm, grad_gain_one = norm_pull_one(grad_normed_one)
    grad_tokens = grad_hidden + grad_tokens_norm
    attn_sums = (
        lax.psum_scatter(grad_qkv, "dp", scatter_dimension=0, tiled=True),
        lax.psum_scatter(grad_attn_out, "dp", scatter_dimension=1, tiled=True),
        lax.psum_scatter(grad_gain_one, "dp", scatter_dimension=0, tiled=True),
    )
    shard_mlp_in, shard_mlp_out, shard_gain_two = mlp_sums
    shard_qkv, shard_attn_out, shard_gain_one = attn_sums
    gain_one_total, gain_two_total = lax.psum((shard_gain_one, shard_gain_two), "tensor")
    return (
        outputs,
        grad_tokens,
        shard_qkv,
        shard_attn_out,
        shard_mlp_in,
        shard_mlp_out,
        gain_one_total,
        gain_two_total,
    )


def solution(mesh):
    in_specs = (
        P(("dp", "tensor"), None),
        P("dp", None),
        P("dp", None, "tensor"),
        P("tensor", "dp"),
        P("dp", None, "tensor"),
        P("tensor", "dp"),
        P("dp"),
        P("dp"),
        P(("dp", "tensor"), None),
    )
    out_specs = (
        P(("dp", "tensor"), None),
        P(("dp", "tensor"), None),
        P("dp", None, "tensor"),
        P("tensor", "dp"),
        P("dp", None, "tensor"),
        P("tensor", "dp"),
        P("dp"),
        P("dp"),
    )
    return jax.shard_map(shards, mesh=mesh, in_specs=in_specs, out_specs=out_specs, check_vma=False)
```

profile of v0, /device:TPU:0, one launch (start us, length us, event | category | flops | bytes accessed | tf_op | source)
XLA Modules:
  0.0 875.3 jit_solution(12923273058877242758)
XLA Ops:
  7.3 1.7 reduce_sum.107
  11.2 43.5 %all-reduce.6 = (bf16[768]{0:T(1024)(128)(2,1)S(1)}, bf16[768]{0:T(1024)(128)(2,1)S(1)}) all-reduce(bf16[768]{0:T(1024)(128)(2,1)S(1)} %dynamic-update-slice, bf16[768]{0:T(1024)(128)(2,1)S(1)} %dynamic-update-slice.1), channel_id=1, replica_groups=mesh['dp'=16,'tensor'=2] {'dp'}, use_global_device_ids=true, to_apply=%add | all-reduce | flops 1536 | bytes 6144
  57.4 41.6 %all_gather.39 = bf16[384,768]{0,1:T(8,128)(2,1)} all-gather(bf16[384,48]{0,1:T(8,128)(2,1)S(1)} %copy-done.31), channel_id=1, replica_groups=mesh['dp'=16,'tensor'=2] {'dp'}, dimensions={1}, use_global_device_ids=true | all-gather | bytes 626688 | tf_op jit(solution)/shard_map/all_gather | solution.py:65
  99.1 25.5 %all-gather.9.cloned.1.call-done = bf16[768,3,384]{2,0,1:T(8,128)(2,1)} async-done(((bf16[48,3,384]{2,0,1:T(8,128)(2,1)}), bf16[768,3,384]{2,0,1:T(8,128)(2,1)}) %all-gather.9.cloned.1.call-update) | async-done | bytes 1769488 | tf_op jit(solution)/shard_map/all_gather | solution.py:64
  124.5 4.0 fusion.68
  132.2 25.0 %while.27 = (s32[]{:T(128)}, bf16[2,512,6,64]{1,3,2,0:T(8,128)(2,1)S(1)}, f32[2,6,512]{2,1,0:T(8,128)S(1)}, s32[2,512]{1,0:T(2,128)S(1)}, s32[1024]{0:T(1024)S(1...) while((s32[]{:T(128)}, ...), condition=%wide.region_6.7_spmd, body=%wide.region_3.6_spmd.sunk | while | flops 843576320 | bytes 42727540 | solution.py:157
  132.6 3.4 fusion.129
  136.0 3.6 fusion.130
  139.6 5.1 fusion.131
  145.1 3.4 fusion.129
  148.5 3.6 fusion.130
  152.2 5.1 fusion.131
  159.1 2.2 convolution_convert_fusion.1
  161.4 2.4 convert_element_type.94
  164.6 4.7 reduce-scatter.9.cloned.1.call-done
  173.0 51.0 %all_gather.43 = bf16[576,768]{0,1:T(8,128)(2,1)} all-gather(bf16[576,48]{0,1:T(8,128)(2,1)S(1)} %copy-done.30), channel_id=1, replica_groups=mesh['dp'=16,'tensor'=2] {'dp'}, dimensions={1}, use_global_device_ids=true | all-gather | bytes 940032 | tf_op jit(solution)/shard_map/all_gather | solution.py:81
  224.1 2.8 fusion.85
  226.9 20.7 %all-gather.13.cloned.1.call-done = bf16[768,2,576]{2,0,1:T(8,128)(2,1)} async-done(((bf16[48,2,576]{2,0,1:T(8,128)(2,1)}), bf16[768,2,576]{2,0,1:T(8,128)(2,1)}) %all-gather.13.cloned.1.call-update) | async-done | bytes 1769488 | tf_op jit(solution)/shard_map/all_gather | solution.py:80
  247.6 10.5 %all-gather.11.cloned.1.call-done = bf16[1024,768]{1,0:T(8,128)(2,1)} async-done(((bf16[512,768]{1,0:T(8,128)(2,1)}), bf16[1024,768]{1,0:T(8,128)(2,1)}) %all-gather.11.cloned.1.call-update) | async-done | bytes 1572880 | tf_op jit(solution)/shard_map/all_gather | solution.py:95
  258.1 4.1 fusion.64
  262.3 5.6 fusion.71
  267.9 2.3 fusion.70
  271.3 3.5 bitcast_convert_fusion.1
  274.9 2.7 convolution_convert_fusion
  277.6 7.6 reduce-scatter.13.cloned.1.call-done
  285.2 2.5 fusion.60
  287.7 10.0 %reduce-scatter.11.cloned.1.call-done = bf16[512,768]{1,0:T(8,128)(2,1)} async-done(((bf16[1024,768]{1,0:T(8,128)(2,1)}), bf16[512,768]{1,0:T(8,128)(2,1)}) %reduce-scatter.11.cloned.1.call-update) | async-done | bytes 786448 | tf_op jit(solution)/shard_map/reduce_scatter | solution.py:107
  297.7 3.1 fusion.81
  303.6 5.8 fusion.62
  309.5 4.8 all-gather.17.cloned.1.call-done
  314.3 3.3 convolution_convert_fusion.2
  320.5 2.2 copy.58
  322.7 89.6 %while.28 = (s32[]{:T(128)}, f32[1024,6,64]{0,2,1:T(8,128)S(1)}, f32[1024,6,64]{0,2,1:T(8,128)}, f32[2,512,6,64]{1,0,3,2:T(2,128)}, bf16[2,512,6,64]{1,3,2,0:T(8...) while((s32[]{:T(128)}, f32[1024,6,64]{0,2,1:T(8,128)S(1)}, ...), condition=%wide.region_16.17_spmd.clone, body=%wide.region_14.16_spmd.clone.sunk | while | flops 2063135744 | bytes 110721200 | solution.py:208
  323.3 2.8 fusion.141
  326.1 5.5 bitcast_add_fusion.5
  331.6 8.4 multiply_reduce_fusion.4
  340.0 7.0 multiply_convert_fusion.6
  347.0 2.0 fusion.142
  349.0 2.4 bitcast_add_fusion.4
  352.2 15.0 %dynamic_update_slice.19 = f32[2,512,6,64]{1,0,3,2:T(2,128)} dynamic-update-slice(f32[2,512,6,64]{1,0,3,2:T(2,128)} %get-tuple-element.475, f32[1,512,6,64]{1,0,3,2:T(1,128)S(1)} %copy.88, s32[]{:T(128)S(6)} %copy.108, s32[]{:T(128)} %constant.64.clone.1..sunk, s32[]{:T(128)} %constant.64.clone.1..sunk, s32[]{:T(128)} %constant.64.clone.1..sunk) | dynamic-update-slice | bytes 1572868 | tf_op jit(solution)/shard_map/while/body/jit(dynamic_update_index_in_dim)/dynamic_update_slice | solution.py:157
  367.6 2.8 fusion.141
  370.5 6.1 bitcast_add_fusion.5
  376.5 8.5 multiply_reduce_fusion.4
  385.0 6.9 multiply_convert_fusion.6
  391.9 2.0 fusion.142
  393.9 2.4 bitcast_add_fusion.4
  397.1 15.0 %dynamic_update_slice.19 = f32[2,512,6,64]{1,0,3,2:T(2,128)} dynamic-update-slice(f32[2,512,6,64]{1,0,3,2:T(2,128)} %get-tuple-element.475, f32[1,512,6,64]{1,0,3,2:T(1,128)S(1)} %copy.88, s32[]{:T(128)S(6)} %copy.108, s32[]{:T(128)} %constant.64.clone.1..sunk, s32[]{:T(128)} %constant.64.clone.1..sunk, s32[]{:T(128)} %constant.64.clone.1..sunk) | dynamic-update-slice | bytes 1572868 | tf_op jit(solution)/shard_map/while/body/jit(dynamic_update_index_in_dim)/dynamic_update_slice | solution.py:157
  412.4 3.5 reshape.252
  415.9 1.8 add_convert_fusion.1
  418.6 1.5 convert.56
  421.3 5.2 bitcast_convert_fusion
  426.6 4.3 fusion.87
  431.0 3.6 fusion.86
  434.6 5.4 fusion.66
  440.8 16.0 %reduce-scatter.21.cloned.1.call-done = f32[48,2,576]{2,0,1:T(8,128)} async-done(((f32[768,2,576]{2,0,1:T(8,128)}), f32[48,2,576]{2,0,1:T(8,128)}) %reduce-scatter.21.cloned.1.call-update) | async-done | bytes 221200 | tf_op jit(solution)/shard_map/reduce_scatter | solution.py:267
  456.8 1.8 copy.65
  458.6 9.5 %reduce-scatter.15.cloned.1.call-done = bf16[512,768]{1,0:T(8,128)(2,1)} async-done(((bf16[1024,768]{1,0:T(8,128)(2,1)}), bf16[512,768]{1,0:T(8,128)(2,1)}) %reduce-scatter.15.cloned.1.call-update) | async-done | bytes 786448 | tf_op jit(solution)/shard_map/reduce_scatter | solution.py:120
  468.1 1.6 fusion.58
  470.6 42.8 %all-reduce.4 = (f32[768]{0:T(1024)S(1)}, f32[768]{0:T(1024)S(1)}) all-reduce(f32[768]{0:T(1024)S(1)} %get-tuple-element.227, f32[768]{0:T(1024)S(1)} %copy-done.38), channel_id=10, replica_groups=mesh['dp'=16,'tensor'=2] {'dp'}, use_global_device_ids=true, to_apply=%region_25.26.clone | all-reduce | flops 1536 | bytes 12288
  513.5 3.0 all-reduce.5
  516.5 3.7 add_add_fusion.2
  520.2 80.6 %reduce-scatter.23.cloned.1.call-done = f32[576,48]{0,1:T(8,128)} async-done(((f32[576,768]{0,1:T(8,128)}), f32[576,48]{0,1:T(8,128)}) %reduce-scatter.23.cloned.1.call-update) | async-done | bytes 110608 | tf_op jit(solution)/shard_map/reduce_scatter | solution.py:268
  600.8 128.6 %reduce-scatter.19.cloned.1.call-done = f32[384,48]{0,1:T(8,128)} async-done(((f32[384,768]{0,1:T(8,128)}), f32[384,48]{0,1:T(8,128)}) %reduce-scatter.19.cloned.1.call-update) | async-done | bytes 73744 | tf_op jit(solution)/shard_map/reduce_scatter | solution.py:307
  729.4 138.9 %reduce-scatter.17.cloned.1.call-done = f32[48,3,384]{2,0,1:T(8,128)} async-done(((f32[768,3,384]{2,0,1:T(8,128)}), f32[48,3,384]{2,0,1:T(8,128)}) %reduce-scatter.17.cloned.1.call-update) | async-done | bytes 221200 | tf_op jit(solution)/shard_map/reduce_scatter | solution.py:306
  (181 shorter events, 27.5 us)
Async XLA Ops:
  7.2 2.2 copy-start.39
  7.2 1.9 copy-start
  7.2 3.5 copy-start.42
  7.2 3.7 copy-start.43
  7.2 91.8 %all-gather.7.cloned.1.call-start = ((), (), s32[]{:S(2)}) async-start(), calls=%async_computation.8 | async-start | bytes 2359296 | tf_op jit(solution)/shard_map/all_gather | solution.py:95
  9.1 46.8 %copy-start.28 = (f32[512]{0:T(512)}, f32[512]{0:T(512)S(1)}, u32[]{:S(2)}) copy-start(f32[512]{0:T(512)S(1)} %broadcast_multiply_fusion.1) | copy-start | bytes 6148
  9.1 47.6 %copy-start.40 = (s32[1,16]{1,0:T(1,128)S(1)}, s32[1,16]{1,0:T(1,128)}, u32[]{:S(2)}) copy-start(s32[1,16]{1,0:T(1,128)} %param.14) | copy-start | bytes 196
  9.1 48.3 %copy-start.31 = (bf16[384,48]{0,1:T(8,128)(2,1)S(1)}, bf16[384,48]{0,1:T(8,128)(2,1)}, u32[]{:S(2)}) copy-start(bf16[384,48]{0,1:T(8,128)(2,1)} %param.16) | copy-start | bytes 110596
  9.4 45.3 %copy-start.36 = (f32[512]{0:T(512)}, f32[512]{0:T(512)S(1)}, u32[]{:S(2)}) copy-start(f32[512]{0:T(512)S(1)} %multiply_reduce_fusion.2) | copy-start | bytes 6148
  9.4 47.4 %copy-start.32 = (f32[512]{0:T(512)}, f32[512]{0:T(512)S(1)}, u32[]{:S(2)}) copy-start(f32[512]{0:T(512)S(1)} %fusion.74) | copy-start | bytes 6148
  54.7 2.1 copy-start.26
  55.9 68.7 %all-gather.9.cloned.1.call-start = ((), (), s32[]{:S(2)}) async-start(), calls=%async_computation.9 | async-start | bytes 1880064 | tf_op jit(solution)/shard_map/all_gather | solution.py:64
  56.6 112.7 %reduce-scatter.9.cloned.1.call-start = ((), (), s32[]{:S(2)}) async-start(), calls=%async_computation.10 | async-start | bytes 2359296 | tf_op jit(solution)/shard_map/reduce_scatter | solution.py:107
  57.4 72.6 %copy-start.12 = (f32[1024,32]{0,1:T(8,128)}, f32[1024,32]{0,1:T(8,128)S(1)}, u32[]{:S(2)}) copy-start(f32[1024,32]{0,1:T(8,128)S(1)} %get-tuple-element.302) | copy-start | bytes 393220
  57.4 72.6 %copy-start.14 = (f32[1024,32]{0,1:T(8,128)}, f32[1024,32]{0,1:T(8,128)S(1)}, u32[]{:S(2)}) copy-start(f32[1024,32]{0,1:T(8,128)S(1)} %get-tuple-element.303) | copy-start | bytes 393220
  157.2 4.0 copy-start.23
  157.3 1.9 copy-start.21
  158.2 0.9 copy-start.18
  161.3 2.5 copy-start.25
  161.3 62.8 %all-gather.15.cloned.1.call-start = ((), (), s32[]{:S(2)}) async-start(), calls=%async_computation.14 | async-start | bytes 2359296 | tf_op jit(solution)/shard_map/all_gather | solution.py:99
  163.8 83.8 %all-gather.13.cloned.1.call-start = ((), (), s32[]{:S(2)}) async-start(), calls=%async_computation.12 | async-start | bytes 2088960 | tf_op jit(solution)/shard_map/all_gather | solution.py:80
  164.5 93.6 %all-gather.11.cloned.1.call-start = ((), (), s32[]{:S(2)}) async-start(), calls=%async_computation.11 | async-start | bytes 2359296 | tf_op jit(solution)/shard_map/all_gather | solution.py:95
  170.7 1.1 copy-start.2
  170.7 2.4 copy-start.30
  173.0 112.2 %reduce-scatter.13.cloned.1.call-start = ((), (), s32[]{:S(2)}) async-start(), calls=%async_computation.15 | async-start | bytes 2359296 | tf_op jit(solution)/shard_map/reduce_scatter | solution.py:120
  267.9 2.3 copy-start.16
  267.9 3.3 copy-start.41
  270.2 1.0 copy-start.10
  271.3 3.6 copy-start.8
  271.3 3.6 copy-start.17
  274.8 22.9 %reduce-scatter.11.cloned.1.call-start = ((), (), s32[]{:S(2)}) async-start(), calls=%async_computation.13 | async-start | bytes 2359296 | tf_op jit(solution)/shard_map/reduce_scatter | solution.py:107
  277.5 7.7 copy-start.3
  277.6 36.7 %all-gather.17.cloned.1.call-start = ((), (), s32[]{:S(2)}) async-start(), calls=%async_computation.16 | async-start | bytes 2359296 | tf_op jit(solution)/shard_map/all_gather | solution.py:99
  285.2 12.5 %copy-start.7 = (bf16[512,768]{1,0:T(8,128)(2,1)S(1)}, bf16[512,768]{1,0:T(8,128)(2,1)}, u32[]{:S(2)}) copy-start(bf16[512,768]{1,0:T(8,128)(2,1)} %reduce-scatter.13.cloned.1.call-done) | copy-start | bytes 2359300
  297.7 4.3 copy-start.4
  300.8 1.2 copy-start.5
  300.8 1.2 copy-start.34
  302.0 1.6 copy-start.11
  303.1 153.7 %reduce-scatter.21.cloned.1.call-start = ((), (), s32[]{:S(2)}) async-start(), calls=%async_computation.20 | async-start | bytes 4177920 | tf_op jit(solution)/shard_map/reduce_scatter | solution.py:267
  309.4 4.9 copy-start.22
  309.4 158.6 %reduce-scatter.15.cloned.1.call-start = ((), (), s32[]{:S(2)}) async-start(), calls=%async_computation.17 | async-start | bytes 2359296 | tf_op jit(solution)/shard_map/reduce_scatter | solution.py:120
  317.6 5.1 copy-start.24
  412.3 3.5 copy-start.13
  412.3 3.5 copy-start.15
  421.3 5.3 copy-start.9
  426.5 4.4 copy-start.19
  426.6 174.3 %reduce-scatter.23.cloned.1.call-start = ((), (), s32[]{:S(2)}) async-start(), calls=%async_computation.21 | async-start | bytes 2088960 | tf_op jit(solution)/shard_map/reduce_scatter | solution.py:268
  430.9 3.7 copy-start.20
  430.9 298.5 %reduce-scatter.19.cloned.1.call-start = ((), (), s32[]{:S(2)}) async-start(), calls=%async_computation.19 | async-start | bytes 1253376 | tf_op jit(solution)/shard_map/reduce_scatter | solution.py:307
  434.6 433.8 %reduce-scatter.17.cloned.1.call-start = ((), (), s32[]{:S(2)}) async-start(), calls=%async_computation.18 | async-start | bytes 3760128 | tf_op jit(solution)/shard_map/reduce_scatter | solution.py:306
  440.0 28.0 %copy-start.1 = (f32[512,768]{1,0:T(8,128)S(1)}, f32[512,768]{1,0:T(8,128)}, u32[]{:S(2)}) copy-start(f32[512,768]{1,0:T(8,128)} %param.13) | copy-start | bytes 4718596
  440.0 28.0 %copy-start.27 = (f32[768]{0:T(1024)S(1)}, f32[768]{0:T(1024)}, u32[]{:S(2)}) copy-start(f32[768]{0:T(1024)} %copy-done.26) | copy-start | bytes 9220
  440.0 28.0 %copy-start.29 = (f32[512]{0:T(512)S(1)}, f32[512]{0:T(512)}, u32[]{:S(2)}) copy-start(f32[512]{0:T(512)} %copy-done.28) | copy-start | bytes 6148
  440.0 29.6 %copy-start.37 = (f32[512]{0:T(512)S(1)}, f32[512]{0:T(512)}, u32[]{:S(2)}) copy-start(f32[512]{0:T(512)} %copy-done.36) | copy-start | bytes 6148
  440.1 29.6 %copy-start.33 = (f32[512]{0:T(512)S(1)}, f32[512]{0:T(512)}, u32[]{:S(2)}) copy-start(f32[512]{0:T(512)} %copy-done.32) | copy-start | bytes 6148
  458.6 12.0 %copy-start.38 = (f32[768]{0:T(1024)S(1)}, f32[768]{0:T(1024)}, u32[]{:S(2)}) copy-start(f32[768]{0:T(1024)} %get-tuple-element.229) | copy-start | bytes 9220
  458.6 57.9 %copy-start.35 = (f32[512]{0:T(512)S(1)}, f32[512]{0:T(512)}, u32[]{:S(2)}) copy-start(f32[512]{0:T(512)} %copy-done.34) | copy-start | bytes 6148
  468.1 1.6 copy-start.6
Sparse Core Ops, SparseCore 0:
  56.0 5.6 all-gather.6
  64.4 60.1 all-gather.8
  161.4 7.8 reduce-scatter.8
  170.8 10.9 all-gather.14
  185.3 62.2 all-gather.12
  249.7 8.4 all-gather.10
  274.9 10.2 reduce-scatter.12
  287.4 10.2 reduce-scatter.10
  303.3 10.9 all-gather.16
  320.1 136.6 reduce-scatter.20
  459.7 8.2 reduce-scatter.14
  473.3 127.4 reduce-scatter.22
  606.9 122.5 reduce-scatter.18
  735.8 132.5 reduce-scatter.16
where the time goes:
time: 888 us; the launch traced here: 875 us
  waiting for transfers between devices  458 us (52%)
  blocking collectives  182 us (20%)
  matrix products  107 us (12%)
  other arithmetic  56.4 us (6%)
  local copies, waits for them, and re-layouts  54.4 us (6%)
  between operations  16.3 us (2%)
    reduce_scatter x1, waiting for transfers between devices, shards(): lax.psum_scatter(grad_qkv, 'dp', scatter_dimension=0, tiled=True)  139 us
    reduce_scatter x1, waiting for transfers between devices, shards(): lax.psum_scatter(grad_attn_out, 'dp', scatter_dimension=1, tiled=True)  129 us
    unnamed x2, blocking collectives  86.3 us
    reduce_scatter x1, waiting for transfers between devices, shards(): lax.psum_scatter(grad_mlp_out, 'dp', scatter_dimension=1, tiled=True)  80.6 us
    all_gather x1, blocking collectives, fetch_mlp(): lax.all_gather(w_mlp_out, 'dp', axis=1, tiled=True)  51 us
    all_gather x1, blocking collectives, fetch_attention(): lax.all_gather(w_attn_out, 'dp', axis=1, tiled=True)  41.6 us
    dynamic_update_slice x4, local copies, waits for them, and re-layouts, attention_forward(): lax.map(one_block, (queries.reshape(block_count, block_rows, heads_here,...  31.7 us
    all_gather x1, waiting for transfers between devices, fetch_attention(): lax.all_gather(w_qkv, 'dp', axis=0, tiled=True)  25.5 us
  transfers between devices with their start and end apart: 14, of which 12 were waited for; matrix products, arithmetic and copies ran while one was open for 18% of the time, Pallas kernels for 0%

commit v1 on v0

--- a/solution.py
+++ b/solution.py
@@ -8,6 +8,18 @@
 EPSILON = 1e-05
 ROPE_BASE = 160000.0
 NEGATIVE = -1e30
+
+
+def doubled_up(shard, axis, dim):
+    ways, here = (lax.axis_size(axis), lax.axis_index(axis))
+    grown, reach = (shard, 1)
+    while reach < ways:
+        theirs = lax.ppermute(grown, axis, [(d, d ^ reach) for d in range(ways)])
+        mine_first = jnp.concatenate([grown, theirs], axis=dim)
+        theirs_first = jnp.concatenate([theirs, grown], axis=dim)
+        grown = jnp.where(here & reach == 0, mine_first, theirs_first)
+        reach = 2 * reach
+    return grown
 
 
 def seq_starts(offset_row, count_rows):
@@ -62,7 +74,7 @@
 def fetch_attention(w_qkv, w_attn_out, gain_attn):
     return (
         lax.all_gather(w_qkv, "dp", axis=0, tiled=True),
-        lax.all_gather(w_attn_out, "dp", axis=1, tiled=True),
+        doubled_up(w_attn_out, "dp", 1),
         lax.all_gather(gain_attn, "dp", axis=0, tiled=True),
     )
 

time: 888 us -> 920 us (1.036)
  waiting for transfers between devices: 458 us -> 482 us
    all_gather x1, waiting for transfers between devices: 25.5 us -> 52.5 us  [fetch_attention(): lax.all_gather(w_qkv, 'dp', axis=0, tiled=True)]
    ppermute x0 -> x4, waiting for transfers between devices: none -> 14.2 us  [doubled_up(): theirs = lax.ppermute(grown, axis, [(d, d ^ reach) for d in range(ways)])]
    reduce_scatter x1, waiting for transfers between devices: 16 us -> 4.33 us  [shards(): lax.psum_scatter(grad_mlp_in, 'dp', scatter_dimension=0, tiled=True)]
  transfers between devices with their start and end apart: 14 -> 18, of which waited for: 12 -> 14; matrix products, arithmetic and copies ran while one was open for 18% -> 21% of each run, Pallas kernels for 0% -> 0%
where the time goes in v1:
time: 920 us; the launch traced here: 907 us
  waiting for transfers between devices  482 us (52%)
  blocking collectives  187 us (20%)
  matrix products  108 us (12%)
  other arithmetic  57.3 us (6%)
  local copies, waits for them, and re-layouts  54.7 us (6%)
  between operations  16.4 us (2%)
    reduce_scatter x1, waiting for transfers between devices, shards(): lax.psum_scatter(grad_qkv, 'dp', scatter_dimension=0, tiled=True)  139 us
    reduce_scatter x1, waiting for transfers between devices, shards(): lax.psum_scatter(grad_attn_out, 'dp', scatter_dimension=1, tiled=True)  129 us
    unnamed x2, blocking collectives  86.2 us
    reduce_scatter x1, waiting for transfers between devices, shards(): lax.psum_scatter(grad_mlp_out, 'dp', scatter_dimension=1, tiled=True)  80.4 us
    all_gather x1, waiting for transfers between devices, fetch_attention(): lax.all_gather(w_qkv, 'dp', axis=0, tiled=True)  52.5 us
    all_gather x1, blocking collectives, fetch_mlp(): lax.all_gather(w_mlp_out, 'dp', axis=1, tiled=True)  51.2 us
    all_gather x1, blocking collectives, fetch_attention_again(): lax.all_gather(w_attn_out, 'dp', axis=1, tiled=True)  46.6 us
    dynamic_update_slice x4, local copies, waits for them, and re-layouts, attention_forward(): lax.map(one_block, (queries.reshape(block_count, block_rows, heads_here,...  31.5 us
  transfers between devices with their start and end apart: 18, of which 14 were waited for; matrix products, arithmetic and copies ran while one was open for 21% of the time, Pallas kernels for 0%

profile of v1, /device:TPU:0, one launch (start us, length us, event | category | flops | bytes accessed | tf_op | source)
XLA Modules:
  0.0 907.4 jit_solution(3288039659741372132)
XLA Ops:
  7.3 1.7 reduce_sum.107
  11.2 43.5 %all-reduce.6 = (bf16[768]{0:T(1024)(128)(2,1)S(1)}, bf16[768]{0:T(1024)(128)(2,1)S(1)}) all-reduce(bf16[768]{0:T(1024)(128)(2,1)S(1)} %dynamic-update-slice, bf16[768]{0:T(1024)(128)(2,1)S(1)} %dynamic-update-slice.1), channel_id=1, replica_groups=mesh['dp'=16,'tensor'=2] {'dp'}, use_global_device_ids=true, to_apply=%add | all-reduce | flops 1536 | bytes 6144
  56.9 3.8 collective-permute-done
  60.8 4.3 collective-permute-done.1
  65.8 6.1 collective-permute-done.2
  72.7 52.5 %all-gather.9.cloned.1.call-done = bf16[768,3,384]{2,0,1:T(8,128)(2,1)} async-done(((bf16[48,3,384]{2,0,1:T(8,128)(2,1)}), bf16[768,3,384]{2,0,1:T(8,128)(2,1)}) %all-gather.9.cloned.1.call-update) | async-done | bytes 1769488 | tf_op jit(solution)/shard_map/all_gather | solution.py:76
  125.2 4.0 fusion.68
  132.8 25.0 %while.27 = (s32[]{:T(128)}, bf16[2,512,6,64]{1,3,2,0:T(8,128)(2,1)S(1)}, f32[2,6,512]{2,1,0:T(8,128)S(1)}, s32[2,512]{1,0:T(2,128)S(1)}, s32[1024]{0:T(1024)S(1...) while((s32[]{:T(128)}, ...), condition=%wide.region_6.7_spmd, body=%wide.region_3.6_spmd.sunk | while | flops 843576320 | bytes 42727540 | solution.py:169
  133.2 3.4 fusion.135
  136.6 3.6 fusion.136
  140.2 5.1 fusion.137
  145.7 3.4 fusion.135
  149.1 3.6 fusion.136
  152.7 5.1 fusion.137
  159.7 3.5 convolution_convert_fusion.1
  163.3 2.4 convert_element_type.94
  166.9 4.4 reduce-scatter.9.cloned.1.call-done
  175.0 51.2 %all_gather.41 = bf16[576,768]{0,1:T(8,128)(2,1)} all-gather(bf16[576,48]{0,1:T(8,128)(2,1)S(1)} %copy-done.30), channel_id=1, replica_groups=mesh['dp'=16,'tensor'=2] {'dp'}, dimensions={1}, use_global_device_ids=true | all-gather | bytes 940032 | tf_op jit(solution)/shard_map/all_gather | solution.py:93
  226.2 2.8 fusion.92
  229.0 20.2 %all-gather.13.cloned.1.call-done = bf16[768,2,576]{2,0,1:T(8,128)(2,1)} async-done(((bf16[48,2,576]{2,0,1:T(8,128)(2,1)}), bf16[768,2,576]{2,0,1:T(8,128)(2,1)}) %all-gather.13.cloned.1.call-update) | async-done | bytes 1769488 | tf_op jit(solution)/shard_map/all_gather | solution.py:92
  249.2 10.5 %all-gather.11.cloned.1.call-done = bf16[1024,768]{1,0:T(8,128)(2,1)} async-done(((bf16[512,768]{1,0:T(8,128)(2,1)}), bf16[1024,768]{1,0:T(8,128)(2,1)}) %all-gather.11.cloned.1.call-update) | async-done | bytes 1572880 | tf_op jit(solution)/shard_map/all_gather | solution.py:107
  259.7 4.1 fusion.64
  263.9 5.6 fusion.71
  269.5 2.3 fusion.70
  272.8 3.5 bitcast_convert_fusion.1
  276.5 2.6 convolution_convert_fusion
  279.2 7.6 reduce-scatter.13.cloned.1.call-done
  286.8 2.5 fusion.60
  289.3 10.0 %reduce-scatter.11.cloned.1.call-done = bf16[512,768]{1,0:T(8,128)(2,1)} async-done(((bf16[1024,768]{1,0:T(8,128)(2,1)}), bf16[512,768]{1,0:T(8,128)(2,1)}) %reduce-scatter.11.cloned.1.call-update) | async-done | bytes 786448 | tf_op jit(solution)/shard_map/reduce_scatter | solution.py:119
  299.3 3.1 fusion.88
  304.8 46.6 %all_gather.44 = bf16[384,768]{0,1:T(8,128)(2,1)} all-gather(bf16[384,48]{0,1:T(8,128)(2,1)} %param.16), channel_id=1, replica_groups=mesh['dp'=16,'tensor'=2] {'dp'}, dimensions={1}, use_global_device_ids=true | all-gather | bytes 626688 | tf_op jit(solution)/shard_map/all_gather | solution.py:85
  351.4 5.8 fusion.62
  358.3 3.3 convolution_convert_fusion.2
  364.5 2.2 copy.58
  366.7 89.5 %while.28 = (s32[]{:T(128)}, f32[1024,6,64]{0,2,1:T(8,128)S(1)}, f32[1024,6,64]{0,2,1:T(8,128)}, f32[2,512,6,64]{1,0,3,2:T(2,128)}, bf16[2,512,6,64]{1,3,2,0:T(8...) while((s32[]{:T(128)}, f32[1024,6,64]{0,2,1:T(8,128)S(1)}, ...), condition=%wide.region_16.17_spmd.clone, body=%wide.region_14.16_spmd.clone.sunk | while | flops 2063135744 | bytes 110721200 | solution.py:220
  367.3 2.8 fusion.147
  370.1 5.5 bitcast_add_fusion.5
  375.6 8.5 multiply_reduce_fusion.4
  384.1 7.0 multiply_convert_fusion.6
  391.1 2.0 fusion.148
  393.1 2.4 bitcast_add_fusion.4
  396.3 14.9 %dynamic_update_slice.19 = f32[2,512,6,64]{1,0,3,2:T(2,128)} dynamic-update-slice(f32[2,512,6,64]{1,0,3,2:T(2,128)} %get-tuple-element.475, f32[1,512,6,64]{1,0,3,2:T(1,128)S(1)} %copy.88, s32[]{:T(128)S(6)} %copy.108, s32[]{:T(128)} %constant.70.clone.1..sunk, s32[]{:T(128)} %constant.70.clone.1..sunk, s32[]{:T(128)} %constant.70.clone.1..sunk) | dynamic-update-slice | bytes 1572868 | tf_op jit(solution)/shard_map/while/body/jit(dynamic_update_index_in_dim)/dynamic_update_slice | solution.py:169
  411.6 2.8 fusion.147
  414.4 6.1 bitcast_add_fusion.5
  420.5 8.5 multiply_reduce_fusion.4
  429.0 6.9 multiply_convert_fusion.6
  435.9 2.0 fusion.148
  437.9 2.4 bitcast_add_fusion.4
  441.1 15.0 %dynamic_update_slice.19 = f32[2,512,6,64]{1,0,3,2:T(2,128)} dynamic-update-slice(f32[2,512,6,64]{1,0,3,2:T(2,128)} %get-tuple-element.475, f32[1,512,6,64]{1,0,3,2:T(1,128)S(1)} %copy.88, s32[]{:T(128)S(6)} %copy.108, s32[]{:T(128)} %constant.70.clone.1..sunk, s32[]{:T(128)} %constant.70.clone.1..sunk, s32[]{:T(128)} %constant.70.clone.1..sunk) | dynamic-update-slice | bytes 1572868 | tf_op jit(solution)/shard_map/while/body/jit(dynamic_update_index_in_dim)/dynamic_update_slice | solution.py:169
  456.2 3.5 reshape.252
  459.7 1.8 add_convert_fusion.1
  465.2 5.2 bitcast_convert_fusion
  470.5 4.3 fusion.94
  474.9 3.6 fusion.93
  478.5 5.4 fusion.66
  484.7 4.3 reduce-scatter.21.cloned.1.call-done
  489.0 1.8 copy.65
  490.8 9.5 %reduce-scatter.15.cloned.1.call-done = bf16[512,768]{1,0:T(8,128)(2,1)} async-done(((bf16[1024,768]{1,0:T(8,128)(2,1)}), bf16[512,768]{1,0:T(8,128)(2,1)}) %reduce-scatter.15.cloned.1.call-update) | async-done | bytes 786448 | tf_op jit(solution)/shard_map/reduce_scatter | solution.py:132
  502.8 42.7 %all-reduce.4 = (f32[768]{0:T(1024)S(1)}, f32[768]{0:T(1024)S(1)}) all-reduce(f32[768]{0:T(1024)S(1)} %get-tuple-element.227, f32[768]{0:T(1024)S(1)} %copy-done.37), channel_id=10, replica_groups=mesh['dp'=16,'tensor'=2] {'dp'}, use_global_device_ids=true, to_apply=%region_25.26.clone | all-reduce | flops 1536 | bytes 12288
  545.7 3.0 all-reduce.5
  548.7 3.7 add_add_fusion.2
  552.4 80.4 %reduce-scatter.23.cloned.1.call-done = f32[576,48]{0,1:T(8,128)} async-done(((f32[576,768]{0,1:T(8,128)}), f32[576,48]{0,1:T(8,128)}) %reduce-scatter.23.cloned.1.call-update) | async-done | bytes 110608 | tf_op jit(solution)/shard_map/reduce_scatter | solution.py:280
  632.8 128.6 %reduce-scatter.19.cloned.1.call-done = f32[384,48]{0,1:T(8,128)} async-done(((f32[384,768]{0,1:T(8,128)}), f32[384,48]{0,1:T(8,128)}) %reduce-scatter.19.cloned.1.call-update) | async-done | bytes 73744 | tf_op jit(solution)/shard_map/reduce_scatter | solution.py:319
  761.4 139.1 %reduce-scatter.17.cloned.1.call-done = f32[48,3,384]{2,0,1:T(8,128)} async-done(((f32[768,3,384]{2,0,1:T(8,128)}), f32[48,3,384]{2,0,1:T(8,128)}) %reduce-scatter.17.cloned.1.call-update) | async-done | bytes 221200 | tf_op jit(solution)/shard_map/reduce_scatter | solution.py:318
  (190 shorter events, 32.6 us)
Async XLA Ops:
  7.2 2.2 copy-start.38
  7.2 1.9 copy-start
  7.2 3.5 copy-start.41
  7.2 3.7 copy-start.42
  7.2 65.5 %all-gather.7.cloned.1.call-start = ((), (), s32[]{:S(2)}) async-start(), calls=%async_computation.8 | async-start | bytes 2359296 | tf_op jit(solution)/shard_map/all_gather | solution.py:107
  9.1 46.8 %copy-start.28 = (f32[512]{0:T(512)}, f32[512]{0:T(512)S(1)}, u32[]{:S(2)}) copy-start(f32[512]{0:T(512)S(1)} %broadcast_multiply_fusion.1) | copy-start | bytes 6148
  9.1 47.6 %copy-start.24 = (bf16[384,48]{0,1:T(8,128)(2,1)S(1)}, bf16[384,48]{0,1:T(8,128)(2,1)}, u32[]{:S(2)}) copy-start(bf16[384,48]{0,1:T(8,128)(2,1)} %param.16) | copy-start | bytes 110596
  9.1 47.7 %copy-start.39 = (s32[1,16]{1,0:T(1,128)S(1)}, s32[1,16]{1,0:T(1,128)}, u32[]{:S(2)}) copy-start(s32[1,16]{1,0:T(1,128)} %param.14) | copy-start | bytes 196
  9.4 45.3 %copy-start.35 = (f32[512]{0:T(512)}, f32[512]{0:T(512)S(1)}, u32[]{:S(2)}) copy-start(f32[512]{0:T(512)S(1)} %multiply_reduce_fusion.2) | copy-start | bytes 6148
  9.4 55.8 %copy-start.31 = (f32[512]{0:T(512)}, f32[512]{0:T(512)S(1)}, u32[]{:S(2)}) copy-start(f32[512]{0:T(512)S(1)} %fusion.80) | copy-start | bytes 6148
  54.7 10.5 %copy-start.26 = (f32[768]{0:T(1024)}, f32[768]{0:T(1024)S(1)}, u32[]{:S(2)}) copy-start(f32[768]{0:T(1024)S(1)} %convert_element_type.81) | copy-start | bytes 9220
  55.9 69.4 %all-gather.9.cloned.1.call-start = ((), (), s32[]{:S(2)}) async-start(), calls=%async_computation.9 | async-start | bytes 1880064 | tf_op jit(solution)/shard_map/all_gather | solution.py:76
  56.6 114.6 %reduce-scatter.9.cloned.1.call-start = ((), (), s32[]{:S(2)}) async-start(), calls=%async_computation.10 | async-start | bytes 2359296 | tf_op jit(solution)/shard_map/reduce_scatter | solution.py:119
  56.7 4.0 collective-permute-start
  60.7 4.4 collective-permute-start.1
  65.2 6.8 collective-permute-start.2
  65.8 64.9 %copy-start.12 = (f32[1024,32]{0,1:T(8,128)}, f32[1024,32]{0,1:T(8,128)S(1)}, u32[]{:S(2)}) copy-start(f32[1024,32]{0,1:T(8,128)S(1)} %get-tuple-element.302) | copy-start | bytes 393220
  65.8 64.9 %copy-start.14 = (f32[1024,32]{0,1:T(8,128)}, f32[1024,32]{0,1:T(8,128)S(1)}, u32[]{:S(2)}) copy-start(f32[1024,32]{0,1:T(8,128)S(1)} %get-tuple-element.303) | copy-start | bytes 393220
  72.7 86.1 %collective-permute-start.3 = (bf16[384,384]{0,1:T(8,128)(2,1)}, bf16[384,384]{0,1:T(8,128)(2,1)}, u32[]{:S(2)}, u32[]{:S(2)}) collective-permute-start(bf16[384,384]{0,1:T(8,128)(2,1)} %maximum_select_fusion.2), channel_id=1, source_target_pairs={{0,16},{2,18},{4,20},{6,22},{8,24},{10,26},{12,28},{14,30},{16,0},... | collective-permute-start | bytes 884744 | tf_op jit(solution)/shard_map/ppermute | solution.py:17
  157.8 5.4 copy-start.22
  158.8 0.9 copy-start.18
  163.2 2.5 copy-start.25
  163.3 62.9 %all-gather.15.cloned.1.call-start = ((), (), s32[]{:S(2)}) async-start(), calls=%async_computation.14 | async-start | bytes 2359296 | tf_op jit(solution)/shard_map/all_gather | solution.py:111
  165.7 83.5 %all-gather.13.cloned.1.call-start = ((), (), s32[]{:S(2)}) async-start(), calls=%async_computation.12 | async-start | bytes 2088960 | tf_op jit(solution)/shard_map/all_gather | solution.py:92
  166.5 93.3 %all-gather.11.cloned.1.call-start = ((), (), s32[]{:S(2)}) async-start(), calls=%async_computation.11 | async-start | bytes 2359296 | tf_op jit(solution)/shard_map/all_gather | solution.py:107
  172.6 1.1 copy-start.2
  172.6 2.3 copy-start.30
  174.9 111.8 %reduce-scatter.13.cloned.1.call-start = ((), (), s32[]{:S(2)}) async-start(), calls=%async_computation.15 | async-start | bytes 2359296 | tf_op jit(solution)/shard_map/reduce_scatter | solution.py:132
  269.5 2.3 copy-start.16
  269.5 3.3 copy-start.40
  271.8 1.0 copy-start.10
  272.8 3.6 copy-start.8
  272.8 3.6 copy-start.17
  276.4 22.9 %reduce-scatter.11.cloned.1.call-start = ((), (), s32[]{:S(2)}) async-start(), calls=%async_computation.13 | async-start | bytes 2359296 | tf_op jit(solution)/shard_map/reduce_scatter | solution.py:119
  279.1 7.7 copy-start.3
  279.1 78.2 %all-gather.17.cloned.1.call-start = ((), (), s32[]{:S(2)}) async-start(), calls=%async_computation.16 | async-start | bytes 2359296 | tf_op jit(solution)/shard_map/all_gather | solution.py:111
  286.8 12.5 %copy-start.7 = (bf16[512,768]{1,0:T(8,128)(2,1)S(1)}, bf16[512,768]{1,0:T(8,128)(2,1)}, u32[]{:S(2)}) copy-start(bf16[512,768]{1,0:T(8,128)(2,1)} %reduce-scatter.13.cloned.1.call-done) | copy-start | bytes 2359300
  299.3 4.3 copy-start.4
  302.4 1.2 copy-start.5
  302.4 1.2 copy-start.33
  303.6 47.9 %copy-start.11 = (bf16[1024,1,576]{0,2,1:T(8,128)(2,1)S(1)}, bf16[1024,1,576]{0,2,1:T(8,128)(2,1)}, u32[]{:S(2)}) copy-start(bf16[1024,1,576]{0,2,1:T(8,128)(2,1)} %copy-done.10) | copy-start | bytes 3538948
  304.7 184.3 %reduce-scatter.21.cloned.1.call-start = ((), (), s32[]{:S(2)}) async-start(), calls=%async_computation.20 | async-start | bytes 4177920 | tf_op jit(solution)/shard_map/reduce_scatter | solution.py:279
  357.3 1.1 copy-start.21
  357.3 143.0 %reduce-scatter.15.cloned.1.call-start = ((), (), s32[]{:S(2)}) async-start(), calls=%async_computation.17 | async-start | bytes 2359296 | tf_op jit(solution)/shard_map/reduce_scatter | solution.py:132
  361.7 5.1 copy-start.23
  456.2 3.5 copy-start.13
  456.2 3.5 copy-start.15
  465.2 5.3 copy-start.9
  470.4 4.4 copy-start.19
  470.4 162.3 %reduce-scatter.23.cloned.1.call-start = ((), (), s32[]{:S(2)}) async-start(), calls=%async_computation.21 | async-start | bytes 2088960 | tf_op jit(solution)/shard_map/reduce_scatter | solution.py:280
  474.8 3.7 copy-start.20
  474.8 286.6 %reduce-scatter.19.cloned.1.call-start = ((), (), s32[]{:S(2)}) async-start(), calls=%async_computation.19 | async-start | bytes 1253376 | tf_op jit(solution)/shard_map/reduce_scatter | solution.py:319
  478.4 422.0 %reduce-scatter.17.cloned.1.call-start = ((), (), s32[]{:S(2)}) async-start(), calls=%async_computation.18 | async-start | bytes 3760128 | tf_op jit(solution)/shard_map/reduce_scatter | solution.py:318
  483.9 16.4 %copy-start.1 = (f32[512,768]{1,0:T(8,128)S(1)}, f32[512,768]{1,0:T(8,128)}, u32[]{:S(2)}) copy-start(f32[512,768]{1,0:T(8,128)} %param.13) | copy-start | bytes 4718596
  483.9 16.4 %copy-start.27 = (f32[768]{0:T(1024)S(1)}, f32[768]{0:T(1024)}, u32[]{:S(2)}) copy-start(f32[768]{0:T(1024)} %copy-done.26) | copy-start | bytes 9220
  483.9 16.4 %copy-start.29 = (f32[512]{0:T(512)S(1)}, f32[512]{0:T(512)}, u32[]{:S(2)}) copy-start(f32[512]{0:T(512)} %copy-done.28) | copy-start | bytes 6148
  483.9 18.0 %copy-start.36 = (f32[512]{0:T(512)S(1)}, f32[512]{0:T(512)}, u32[]{:S(2)}) copy-start(f32[512]{0:T(512)} %copy-done.35) | copy-start | bytes 6148
  483.9 18.0 %copy-start.32 = (f32[512]{0:T(512)S(1)}, f32[512]{0:T(512)}, u32[]{:S(2)}) copy-start(f32[512]{0:T(512)} %copy-done.31) | copy-start | bytes 6148
  490.8 12.0 %copy-start.37 = (f32[768]{0:T(1024)S(1)}, f32[768]{0:T(1024)}, u32[]{:S(2)}) copy-start(f32[768]{0:T(1024)} %get-tuple-element.229) | copy-start | bytes 9220
  490.8 57.9 %copy-start.34 = (f32[512]{0:T(512)S(1)}, f32[512]{0:T(512)}, u32[]{:S(2)}) copy-start(f32[512]{0:T(512)} %copy-done.33) | copy-start | bytes 6148
  500.3 1.6 copy-start.6
Sparse Core Ops, SparseCore 0:
  56.0 5.6 all-gather.6
  64.4 60.8 all-gather.8
  163.4 7.8 reduce-scatter.8
  172.7 10.9 all-gather.14
  187.2 61.9 all-gather.12
  251.2 8.4 all-gather.10
  276.5 10.2 reduce-scatter.12
  289.0 10.2 reduce-scatter.10
  304.8 10.9 all-gather.16
  357.4 131.5 reduce-scatter.20
  491.9 8.2 reduce-scatter.14
  505.6 127.1 reduce-scatter.22
  638.8 122.5 reduce-scatter.18
  767.7 132.7 reduce-scatter.16
